TPU v7x, 32 devices: a whole 2x2x4 slice. The times are simulated.
32 devices in a mesh: row: 4 (over y, x), seq: 8 (over z, core).
Axes of the slice: x: 2, y: 2, z: 4, core: 2. Of those that a mesh axis runs over, the one named last changes fastest.
Arguments:
- tokens: bfloat16 [16, 2048, 2048], P('row', 'seq'), may hold values from -6 to 6
- lengths: int32 [16], P('row'), may hold values from 64 to 2048, as said below
- cotangent: bfloat16 [16, 2048, 2048], P('row', 'seq'), may hold values from -6 to 6
- w_qkv: bfloat16 [2048, 1536], P(('row', 'seq')), may hold values from -0.125 to 0.125
- w_out: bfloat16 [2048, 1024], P(('row', 'seq')), may hold values from -1.5 to 1.5
- w_gateup: bfloat16 [2048, 2048], P(('row', 'seq')), may hold values from -0.125 to 0.125
- w_down: bfloat16 [2048, 1024], P(('row', 'seq')), may hold values from -0.1875 to 0.1875
- norm_attn: bfloat16 [2048], P(('row', 'seq')), may hold values from 0.5 to 1.5
- norm_ffn: bfloat16 [2048], P(('row', 'seq')), may hold values from 0.5 to 1.5
- q_gain: bfloat16 [64], replicated, may hold values from 0.099609375 to 1.8984375
- k_gain: bfloat16 [64], replicated, may hold values from 0.099609375 to 1.8984375
Outputs:
- output: bfloat16 [16, 2048, 2048], P('row', 'seq')
- grad_tokens: bfloat16 [16, 2048, 2048], P('row', 'seq')
- grad_qkv: float32 [2048, 1536], P(('row', 'seq'))
- grad_out: float32 [2048, 1024], P(('row', 'seq'))
- grad_gateup: float32 [2048, 2048], P(('row', 'seq'))
- grad_down: float32 [2048, 1024], P(('row', 'seq'))
- grad_norm_attn: float32 [2048], P(('row', 'seq'))
- grad_norm_ffn: float32 [2048], P(('row', 'seq'))
- grad_q_gain: float32 [64], replicated
- grad_k_gain: float32 [64], replicated
Inputs may be any that keep to these rules, and one draw needn't show every extreme that they name: `lengths`: each aligned block of 4 entries (the sequences of one index of row) holds at least one entry equal to 2048; the others are heavy-tailed.
All inputs are finite; a program needn't handle non-finite values.
Results may differ from a plain program's by a relative error of at most 0.033.
Values may be sent and summed in bfloat16 or wider, within the bound.
No kernel may reach another device: no remote copies, remote signals or barrier semaphores. Data moves between devices by JAX's collectives and lax.ppermute only.
A program may use at most 448 MiB of HBM per device.

v0:
```python
import jax
import jax.numpy as jnp
from jax import lax
from jax.sharding import PartitionSpec as P

norm_eps = 1e-06
theta_base = 10000.0
neg_big = -1e30


def rms_norm(values, gain_vec):
    return (
        values * lax.rsqrt(jnp.mean(values * values, axis=-1, keepdims=True) + norm_eps) * gain_vec
    )


def rotate(values, cosine_table, sine_table):
    half_dim = values.shape[-1] // 2
    first_half = values[..., :half_dim]
    second_half = values[..., half_dim:]
    return jnp.concatenate(
        [
            first_half * cosine_table - second_half * sine_table,
            second_half * cosine_table + first_half * sine_table,
        ],
        axis=-1,
    )


def contract_rows(left, right):
    return lax.dot_general(
        left, right, (((0,), (0,)), ((), ())), preferred_element_type=jnp.float32
    )


def times_transposed(left, right):
    return lax.dot_general(
        left, right, (((1,), (1,)), ((), ())), preferred_element_type=jnp.float32
    )


def rounded(values):
    return lax.optimization_barrier(values.astype(jnp.bfloat16)).astype(jnp.float32)


def shards(
    tokens, lengths, cotangent, w_qkv, w_out, w_gateup, w_down, norm_attn, norm_ffn, q_gain, k_gain
):
    seq_count, span_len, model_width = tokens.shape
    row_count = seq_count * span_len
    head_dim = q_gain.shape[0]
    half_dim = head_dim // 2
    query_width = w_out.shape[1]
    kv_width = (w_qkv.shape[1] - query_width) // 2
    kv_heads = kv_width // head_dim
    group_size = query_width // head_dim // kv_heads
    hidden_width = w_down.shape[1]
    score_scale = head_dim ** (-0.5)
    positions = lax.axis_index("seq") * span_len + jnp.arange(span_len, dtype=jnp.int32)
    inverse = theta_base ** (-jnp.arange(half_dim, dtype=jnp.float32) * 2.0 / head_dim)
    angles = positions.astype(jnp.float32)[:, None] * inverse[None, :]
    cosine_table = jnp.cos(angles)[:, None, :]
    sine_table = jnp.sin(angles)[:, None, :]
    gathered = (
        lax.all_gather(w_qkv, ("row", "seq"), axis=0, tiled=True),
        lax.all_gather(w_out, ("row", "seq"), axis=0, tiled=True),
        lax.all_gather(w_gateup, ("row", "seq"), axis=0, tiled=True),
        lax.all_gather(w_down, ("row", "seq"), axis=0, tiled=True),
        lax.all_gather(norm_attn, ("row", "seq"), axis=0, tiled=True),
        lax.all_gather(norm_ffn, ("row", "seq"), axis=0, tiled=True),
    )
    qkv_full, out_full, gateup_full, down_full, attn_gain, ffn_gain = gathered
    attn_gain_f = attn_gain.astype(jnp.float32)
    ffn_gain_f = ffn_gain.astype(jnp.float32)
    query_gain = q_gain.astype(jnp.float32)
    key_gain = k_gain.astype(jnp.float32)

    def head_shape(raw_heads, gain_vec):
        return rotate(rms_norm(raw_heads, gain_vec), cosine_table, sine_table)

    inputs_rows = tokens.reshape(row_count, model_width).astype(jnp.float32)
    normed_attn = rms_norm(inputs_rows, attn_gain_f).astype(jnp.bfloat16)
    projected = jnp.dot(normed_attn, qkv_full, preferred_element_type=jnp.float32)
    query_raw = projected[:, :query_width].reshape(
        seq_count, span_len, kv_heads * group_size, head_dim
    )
    key_raw = projected[:, query_width : query_width + kv_width].reshape(
        seq_count, span_len, kv_heads, head_dim
    )
    query_heads = head_shape(query_raw, query_gain).astype(jnp.bfloat16)
    query_heads = query_heads.reshape(seq_count, span_len, kv_heads, group_size, head_dim)
    key_heads = (
        head_shape(key_raw, key_gain).astype(jnp.bfloat16).reshape(seq_count, span_len, kv_width)
    )
    value_heads = (
        projected[:, query_width + kv_width :]
        .astype(jnp.bfloat16)
        .reshape(seq_count, span_len, kv_width)
    )

    def allowed_at(piece_len):
        key_pos = jnp.arange(piece_len, dtype=jnp.int32)
        causal = key_pos[None, None, :] <= positions[None, :, None]
        inside = key_pos[None, None, :] < lengths[:, None, None]
        return (causal & inside)[:, :, None, None, :]

    def score_piece(key_part):
        key_split = key_part.reshape(seq_count, -1, kv_heads, head_dim)
        scores = jnp.einsum(
            "sqkgd,snkd->sqkgn", query_heads, key_split, preferred_element_type=jnp.float32
        )
        return scores * score_scale

    stat_shape = (seq_count, span_len, kv_heads, group_size)
    run_max = jnp.full(stat_shape, neg_big, jnp.float32)
    key_part = lax.all_gather(key_heads, "seq", axis=1, tiled=True)
    value_part = lax.all_gather(value_heads, "seq", axis=1, tiled=True)
    piece_len = key_part.shape[1]
    scores = score_piece(key_part)
    allowed = allowed_at(piece_len)
    new_max = jnp.maximum(run_max, jnp.max(jnp.where(allowed, scores, neg_big), axis=-1))
    weights_now = jnp.where(allowed, jnp.exp(scores - new_max[..., None]), 0.0)
    value_split = value_part.reshape(seq_count, piece_len, kv_heads, head_dim)
    added = jnp.einsum(
        "sqkgn,snkd->sqkgd",
        weights_now.astype(jnp.bfloat16),
        value_split,
        preferred_element_type=jnp.float32,
    )
    run_sum = jnp.sum(weights_now, axis=-1)
    out_heads = added / run_sum[..., None]
    log_total = new_max + jnp.log(run_sum)
    attended = out_heads.reshape(row_count, query_width).astype(jnp.bfloat16)
    middle = inputs_rows + times_transposed(attended, out_full)
    normed_ffn = rms_norm(middle, ffn_gain_f).astype(jnp.bfloat16)
    gate_up = jnp.dot(normed_ffn, gateup_full, preferred_element_type=jnp.float32)
    gate_part = gate_up[:, :hidden_width]
    up_part = gate_up[:, hidden_width:]
    sigmoid_gate = jax.nn.sigmoid(gate_part)
    silu_gate = gate_part * sigmoid_gate
    hidden = (silu_gate * up_part).astype(jnp.bfloat16)
    result = middle + times_transposed(hidden, down_full)
    output = result.astype(jnp.bfloat16).reshape(seq_count, span_len, model_width)
    again = (
        lax.all_gather(w_qkv, ("row", "seq"), axis=0, tiled=True),
        lax.all_gather(w_out, ("row", "seq"), axis=0, tiled=True),
        lax.all_gather(w_gateup, ("row", "seq"), axis=0, tiled=True),
        lax.all_gather(w_down, ("row", "seq"), axis=0, tiled=True),
        lax.all_gather(norm_attn, ("row", "seq"), axis=0, tiled=True),
        lax.all_gather(norm_ffn, ("row", "seq"), axis=0, tiled=True),
    )
    qkv_back, out_back, gateup_back, down_back, attn_gain_b, ffn_gain_b = again
    row_valid = (positions[None, :] < lengths[:, None]).astype(jnp.float32).reshape(row_count, 1)
    grad_rows = cotangent.reshape(row_count, model_width).astype(jnp.float32) * row_valid
    grad_branch = grad_rows.astype(jnp.bfloat16)
    grad_down = contract_rows(grad_branch, hidden)
    grad_hidden = jnp.dot(grad_branch, down_back, preferred_element_type=jnp.float32)
    grad_gate = grad_hidden * up_part * (sigmoid_gate * (1.0 + gate_part * (1.0 - sigmoid_gate)))
    grad_up = grad_hidden * silu_gate
    grad_gate_up = jnp.concatenate([grad_gate, grad_up], axis=1).astype(jnp.bfloat16)
    grad_gateup_w = contract_rows(normed_ffn, grad_gate_up)
    grad_normed_ffn = times_transposed(grad_gate_up, gateup_back)
    unused_ffn, ffn_pull = jax.vjp(rms_norm, middle, ffn_gain_b.astype(jnp.float32))
    grad_mid_norm, grad_ffn_gain = ffn_pull(grad_normed_ffn)
    grad_middle = grad_rows + grad_mid_norm
    grad_attn_branch = grad_middle.astype(jnp.bfloat16)
    grad_out_w = contract_rows(grad_attn_branch, attended)
    grad_attended = jnp.dot(grad_attn_branch, out_back, preferred_element_type=jnp.float32).astype(
        jnp.bfloat16
    )
    grad_heads = grad_attended.reshape(seq_count, span_len, kv_heads, group_size, head_dim)
    row_dot = jnp.sum(grad_heads.astype(jnp.float32) * out_heads, axis=-1)
    key_part = lax.all_gather(key_heads, "seq", axis=1, tiled=True)
    value_part = lax.all_gather(value_heads, "seq", axis=1, tiled=True)
    piece_len = key_part.shape[1]
    scores = score_piece(key_part)
    allowed = allowed_at(piece_len)
    probabilities = jnp.where(allowed, jnp.exp(scores - log_total[..., None]), 0.0)
    value_split = value_part.reshape(seq_count, piece_len, kv_heads, head_dim)
    key_split = key_part.reshape(seq_count, piece_len, kv_heads, head_dim)
    grad_probs = jnp.einsum(
        "sqkgd,snkd->sqkgn", grad_heads, value_split, preferred_element_type=jnp.float32
    )
    grad_scores = (probabilities * (grad_probs - row_dot[..., None])).astype(jnp.bfloat16)
    grad_query_acc = score_scale * jnp.einsum(
        "sqkgn,snkd->sqkgd", grad_scores, key_split, preferred_element_type=jnp.float32
    )
    grad_keys = score_scale * jnp.einsum(
        "sqkgn,sqkgd->snkd", grad_scores, query_heads, preferred_element_type=jnp.float32
    )
    grad_values = jnp.einsum(
        "sqkgn,sqkgd->snkd",
        probabilities.astype(jnp.bfloat16),
        grad_heads,
        preferred_element_type=jnp.float32,
    )
    update = jnp.concatenate(
        [
            grad_keys.reshape(seq_count, piece_len, kv_width),
            grad_values.reshape(seq_count, piece_len, kv_width),
        ],
        axis=-1,
    )
    grad_kv_all = update
    grad_query_acc, grad_kv_all = (grad_query_acc, grad_kv_all)
    grad_kv = lax.psum_scatter(
        grad_kv_all.astype(jnp.bfloat16), "seq", scatter_dimension=1, tiled=True
    ).astype(jnp.float32)
    grad_key_heads = rounded(grad_kv[..., :kv_width]).reshape(
        seq_count, span_len, kv_heads, head_dim
    )
    grad_value = rounded(grad_kv[..., kv_width:]).reshape(row_count, kv_width)
    grad_query_heads = rounded(grad_query_acc).reshape(
        seq_count, span_len, kv_heads * group_size, head_dim
    )
    unused_query, query_pull = jax.vjp(head_shape, query_raw, query_gain)
    grad_query_raw, grad_q_part = query_pull(grad_query_heads)
    unused_key, key_pull = jax.vjp(head_shape, key_raw, key_gain)
    grad_key_raw, grad_k_part = key_pull(grad_key_heads)
    grad_projected = jnp.concatenate(
        [
            grad_query_raw.reshape(row_count, query_width),
            grad_key_raw.reshape(row_count, kv_width),
            grad_value,
        ],
        axis=1,
    ).astype(jnp.bfloat16)
    grad_qkv_w = contract_rows(normed_attn, grad_projected)
    grad_normed_attn = times_transposed(grad_projected, qkv_back)
    unused_attn, attn_pull = jax.vjp(rms_norm, inputs_rows, attn_gain_b.astype(jnp.float32))
    grad_in_norm, grad_attn_gain = attn_pull(grad_normed_attn)
    grad_tokens = (
        (grad_middle + grad_in_norm).astype(jnp.bfloat16).reshape(seq_count, span_len, model_width)
    )
    summed = (
        lax.psum_scatter(grad_qkv_w, ("row", "seq"), scatter_dimension=0, tiled=True),
        lax.psum_scatter(grad_out_w, ("row", "seq"), scatter_dimension=0, tiled=True),
        lax.psum_scatter(grad_gateup_w, ("row", "seq"), scatter_dimension=0, tiled=True),
        lax.psum_scatter(grad_down, ("row", "seq"), scatter_dimension=0, tiled=True),
        lax.psum_scatter(grad_attn_gain, ("row", "seq"), scatter_dimension=0, tiled=True),
        lax.psum_scatter(grad_ffn_gain, ("row", "seq"), scatter_dimension=0, tiled=True),
    )
    gain_sums = lax.psum((grad_q_part, grad_k_part), ("row", "seq"))
    return (
        output,
        grad_tokens,
        summed[0],
        summed[1],
        summed[2],
        summed[3],
        summed[4],
        summed[5],
        gain_sums[0],
        gain_sums[1],
    )


def solution(mesh):
    placed = (
        P("row", "seq", None),
        P("row"),
        P("row", "seq", None),
        P(("row", "seq"), None),
        P(("row", "seq"), None),
        P(("row", "seq"), None),
        P(("row", "seq"), None),
        P(("row", "seq")),
        P(("row", "seq")),
        P(),
        P(),
    )
    return jax.shard_map(
        shards,
        mesh=mesh,
        in_specs=placed,
        out_specs=(
            P("row", "seq", None),
            P("row", "seq", None),
            P(("row", "seq"), None),
            P(("row", "seq"), None),
            P(("row", "seq"), None),
            P(("row", "seq"), None),
            P(("row", "seq")),
            P(("row", "seq")),
            P(),
            P(),
        ),
        check_vma=False,
    )
```

profile of v0, /device:TPU:0, one launch (start us, length us, event | category | flops | bytes accessed | tf_op | source)
XLA Modules:
  0.0 1375.0 jit_solution(15780627546519049611)
XLA Ops:
  12.9 42.3 %all-reduce.9 = (bf16[2048]{0:T(1024)(128)(2,1)S(1)}, bf16[2048]{0:T(1024)(128)(2,1)S(1)}) all-reduce(bf16[2048]{0:T(1024)(128)(2,1)S(1)} %dynamic-update-slice, bf16[2048]{0:T(1024)(128)(2,1)S(1)} %dynamic-update-slice.1), channel_id=1, replica_groups=mesh['row'=4,'seq'=8] {'row','seq'}, use_global_device_ids=true, to_apply=%add.4 | all-reduce | flops 4096 | bytes 16384
  60.8 22.8 %all-gather.7.cloned.1.call-done = bf16[2048,1536]{1,0:T(8,128)(2,1)} async-done(((bf16[64,1536]{1,0:T(8,128)(2,1)}), bf16[2048,1536]{1,0:T(8,128)(2,1)}) %all-gather.7.cloned.1.call-update) | async-done | bytes 6291472 | tf_op jit(solution)/shard_map/all_gather | solution.py:65
  132.8 12.9 all-gather.11.cloned.1.call-done
  145.8 47.4 %fusion.2 = (f32[4,256,4,4]{1,3,2,0:T(4,128)S(1)}, f32[4,4,2048,256,4]{3,2,4,1,0:T(8,128)}) fusion(pred[4,256,2048]{1,2,0:T(8,128)(4,1)S(1)} %broadcast_and_fusion, bf16[4,2048,4,64,1]{1,3,4,2,0:T(8,128)(2,1)} %bitcast.148, bf16[4,256,4,4,32]{1,4,3,2,0:T(8,128)(2,1)} %bitcast.153, bf16[4,256,4,4,32]{1,4,3,2,0:T(8,128)(2,1)S(1)} %bitcast.151), kind=kOutput, calls=%fused_computation.6 | convolution fusion | flops 4399808512 | bytes 142671872 | tf_op jit(solution)/shard_map/sqkgd,snkd->sqkgn/dot_general | solution.py:109
  193.2 41.3 %fusion.8 = f32[4,256,4,4]{1,3,2,0:T(4,128)S(1)} fusion(f32[4,4,2048,256,4]{3,2,4,1,0:T(8,128)} %get-tuple-element.44, f32[4,256,4,4]{1,3,2,0:T(4,128)S(1)} %broadcast_maximum_fusion, pred[4,256,2048]{1,2,0:T(8,128)(4,1)S(1)} %broadcast_and_fusion), kind=kLoop, calls=%fused_computation.12 | loop fusion | flops 134201344 | bytes 136445952 | tf_op jit(solution)/shard_map/reduce_sum | solution.py:130
  241.1 48.3 %fusion.65 = (bf16[4,256,4,4,64]{1,4,3,2,0:T(8,128)(2,1)}, f32[4,256,4,4,64]{1,4,3,2,0:T(8,128)}) fusion(f32[4,256,4,4]{1,3,2,0:T(4,128)S(1)} %fusion.8, bf16[4,2048,4,64,1]{1,3,4,2,0:T(8,128)(2,1)} %bitcast.160, f32[4,4,2048,256,4]{3,2,4,1,0:T(8,128)} %get-tuple-element.44, f32[4,256,4,4]{1,3,2,0:T(4,128)S(1)} %broadcast_maximum_fusion, ...), kind=kOutput, calls=%fused_computation.127 | convolution fusion | flops 4431282176 | bytes 146931712 | tf_op jit(solution)/shard_map/sqkgn,snkd->sqkgd/dot_general | solution.py:124
  294.6 12.8 multiply_reduce_fusion.2
  307.4 27.9 %all-gather.15.cloned.1.call-done = bf16[2048,2048]{1,0:T(8,128)(2,1)} async-done(((bf16[64,2048]{1,0:T(8,128)(2,1)}), bf16[2048,2048]{1,0:T(8,128)(2,1)}) %all-gather.15.cloned.1.call-update) | async-done | bytes 8388624 | tf_op jit(solution)/shard_map/all_gather | solution.py:67
  335.3 16.0 %fusion.61 = f32[1024,2048]{1,0:T(8,128)} fusion(bf16[2048,2048]{1,0:T(8,128)(2,1)} %all-gather.15.cloned.1.call-done, f32[1024,2048]{1,0:T(8,128)} %get-tuple-element.48, f32[2048]{0:T(1024)S(1)} %copy-done.34, f32[1024]{0:T(1024)S(1)} %fusion.49), kind=kOutput, calls=%fused_computation.123 | convolution fusion | flops 8596226048 | bytes 25178112 | tf_op jit(solution)/shard_map/dot_general | solution.py:136
  351.3 47.6 %all-gather.17.cloned.1.call-done = bf16[2048,1024]{1,0:T(8,128)(2,1)} async-done(((bf16[64,1024]{1,0:T(8,128)(2,1)}), bf16[2048,1024]{1,0:T(8,128)(2,1)}) %all-gather.17.cloned.1.call-update) | async-done | bytes 4194320 | tf_op jit(solution)/shard_map/all_gather | solution.py:68
  398.9 14.4 %multiply_convert_fusion.3 = (bf16[1024,1024]{1,0:T(8,128)(2,1)}, bf16[1024,1024]{1,0:T(8,128)(2,1)}, bf16[1024,1024]{1,0:T(8,128)(2,1)}) fusion(f32[1024,2048]{1,0:T(8,128)} %fusion.61, bf16[1024,2048]{1,0:T(8,128)(2,1)} %fusion.19, bf16[2048,1024]{1,0:T(8,128)(2,1)} %all-gather.17.cloned.1.call-done), kind=kOutput, calls=%fused_computation.55 | convolution fusion | flops 4310695936 | bytes 23068672 | tf_op jit(solution)/shard_map/dot_general | solution.py:157
  413.4 17.5 %multiply_reduce_fusion = (f32[2048]{0:T(1024)}, f32[1024]{0:T(1024)S(1)}, f32[1024,2048]{1,0:T(8,128)}) fusion(f32[1024,2048]{1,0:T(8,128)} %get-tuple-element.48, f32[1024]{0:T(1024)S(1)} %fusion.49, f32[2048]{0:T(1024)S(1)} %copy-done.34, bf16[2048,2048]{1,0:T(8,128)(2,1)} %all-gather.15.cloned.1.call-done, bf16[1024,1024]{1,0:T(8,128)(2,1)} %get-tuple-element.25, ...), kind=kOutput, calls=%fused_computation.40 | convolution fusion | flops 8610903040 | bytes 29384704 | tf_op jit(solution)/shard_map/dot_general | solution.py:37
  468.4 45.4 %bitcast_convert_fusion = bf16[4,4,64,2048]{3,2,1,0:T(8,128)(2,1)} fusion(bf16[4,256,4,4,64]{1,4,3,2,0:T(8,128)(2,1)} %copy.68, f32[4,4,2048,256,4]{3,2,4,1,0:T(8,128)} %get-tuple-element.44, f32[4,256,4,4]{1,3,2,0:T(4,128)S(1)} %log_add_fusion, pred[4,256,2048]{1,2,0:T(8,128)(4,1)S(1)} %broadcast_and_fusion), kind=kOutput, calls=%fused_computation.26 | convolution fusion | flops 4431282176 | bytes 142671872 | tf_op jit(solution)/shard_map/sqkgn,sqkgd->snkd/dot_general | solution.py:191
  513.9 74.3 %fusion.1 = bf16[4,256,4,4,2048]{1,4,3,2,0:T(8,128)(2,1)} fusion(f32[4,4,2048,256,4]{3,2,4,1,0:T(8,128)} %get-tuple-element.44, bf16[4,2048,4,64,1]{1,3,4,2,0:T(8,128)(2,1)} %bitcast.161, bf16[4,256,4,4,64]{1,4,3,2,0:T(8,128)(2,1)} %copy.68, f32[4,256,4,4]{1,3,2,0:T(4,128)S(1)} %multiply_reduce_fusion.5, f32[4,256,4,4]{1,3,2,0:T(4,128)S(1)} %log_add_fusion, ...), kind=kOutput, calls=%fused_computation.2 | convolution fusion | flops 4496293888 | bytes 209846272 | tf_op jit(solution)/shard_map/sqkgd,snkd->sqkgn/dot_general | solution.py:181
  588.1 31.2 %fusion.20 = bf16[4,4,64,2048]{3,2,1,0:T(8,128)(2,1)} fusion(bf16[4,256,4,4,2048]{1,4,3,2,0:T(8,128)(2,1)} %fusion.1, bf16[4,256,4,4,32]{1,4,3,2,0:T(8,128)(2,1)} %bitcast.154, bf16[4,256,4,4,32]{1,4,3,2,0:T(8,128)(2,1)S(1)} %bitcast.152), kind=kOutput, calls=%fused_computation.28 | convolution fusion | flops 4303355904 | bytes 73400320 | tf_op jit(solution)/shard_map/sqkgn,sqkgd->snkd/dot_general | solution.py:188
  652.0 16.6 %fusion.31 = f32[2048,2048]{1,0:T(8,128)} fusion(bf16[1024,1024]{1,0:T(8,128)(2,1)} %get-tuple-element.25, bf16[1024,1024]{1,0:T(8,128)(2,1)S(1)} %copy-done.49, f32[1024,2048]{1,0:T(8,128)} %get-tuple-element.48, f32[2048]{0:T(1024)S(1)} %copy-done.35, f32[1024]{0:T(1024)S(1)} %copy-done.37), kind=kOutput, calls=%fused_computation.63 | convolution fusion | flops 8604614656 | bytes 29372416 | tf_op jit(solution)/shard_map/dot_general | solution.py:31
  668.8 25.3 %fusion.42 = bf16[4,256,4,4,64]{1,4,3,2,0:T(8,128)(2,1)S(1)} fusion(bf16[4,2048,4,64,1]{1,3,4,2,0:T(8,128)(2,1)} %bitcast.149, bf16[4,256,4,4,2048]{1,4,3,2,0:T(8,128)(2,1)} %fusion.1), kind=kOutput, calls=%fused_computation.76 | convolution fusion | flops 4297064448 | bytes 73400320 | tf_op jit(solution)/shard_map/sqkgn,snkd->sqkgd/dot_general | solution.py:185
  732.9 12.0 add_convert_fusion
  745.0 13.2 fusion.24
  758.2 39.1 %all-reduce.8 = (f32[2048]{0:T(1024)S(1)}, f32[2048]{0:T(1024)S(1)}, f32[64]{0:T(128)}, f32[64]{0:T(128)}) all-reduce(f32[2048]{0:T(1024)S(1)} %get-tuple-element.12, f32[2048]{0:T(1024)S(1)} %copy-done.38, f32[64]{0:T(128)S(1)} %get-tuple-element.14, f32[64]{0:T(128)S(1)} %get-tuple-element.16), channel_id=7, replica_groups=mesh['row'=4,'seq'=8] {'row','seq'}, use_global_device_ids=true, to_apply=%region_17.18.clone | all-reduce | flops 4224 | bytes 33792
  808.9 60.4 %reduce-scatter.14.cloned.1.call-done = f32[64,1024]{1,0:T(8,128)} async-done(((f32[2048,1024]{1,0:T(8,128)}), f32[64,1024]{1,0:T(8,128)}) %reduce-scatter.14.cloned.1.call-update) | async-done | bytes 262160 | tf_op jit(solution)/shard_map/reduce_scatter | solution.py:239
  869.3 152.2 %reduce-scatter.10.cloned.1.call-done = f32[64,1024]{1,0:T(8,128)} async-done(((f32[2048,1024]{1,0:T(8,128)}), f32[64,1024]{1,0:T(8,128)}) %reduce-scatter.10.cloned.1.call-update) | async-done | bytes 262160 | tf_op jit(solution)/shard_map/reduce_scatter | solution.py:237
  1021.4 187.2 %reduce-scatter.12.cloned.1.call-done = f32[64,2048]{1,0:T(8,128)} async-done(((f32[2048,2048]{1,0:T(8,128)}), f32[64,2048]{1,0:T(8,128)}) %reduce-scatter.12.cloned.1.call-update) | async-done | bytes 524304 | tf_op jit(solution)/shard_map/reduce_scatter | solution.py:238
  1208.6 159.7 %reduce-scatter.8.cloned.1.call-done = f32[64,1536]{1,0:T(8,128)} async-done(((f32[2048,1536]{1,0:T(8,128)}), f32[64,1536]{1,0:T(8,128)}) %reduce-scatter.8.cloned.1.call-update) | async-done | bytes 393232 | tf_op jit(solution)/shard_map/reduce_scatter | solution.py:236
  (207 shorter events, 192.3 us)
Async XLA Ops:
  7.2 76.4 %all-gather.7.cloned.1.call-start = ((), (), s32[]{:S(2)}) async-start(), calls=%async_computation.5 | async-start | bytes 6488064 | tf_op jit(solution)/shard_map/all_gather | solution.py:65
  7.9 137.8 %all-gather.11.cloned.1.call-start = ((), (), s32[]{:S(2)}) async-start(), calls=%async_computation.7 | async-start | bytes 4718592 | tf_op jit(solution)/shard_map/all_gather | solution.py:116
  8.6 88.8 %copy-start.41 = (f32[64]{0:T(128)}, f32[64]{0:T(128)S(1)}, u32[]{:S(2)}) copy-start(f32[64]{0:T(128)S(1)} %convert_element_type.116) | copy-start | bytes 772
  12.3 48.4 %copy-start.32 = (f32[1024]{0:T(1024)}, f32[1024]{0:T(1024)S(1)}, u32[]{:S(2)}) copy-start(f32[1024]{0:T(1024)S(1)} %rsqrt.44) | copy-start | bytes 12292
  55.4 74.8 %copy-start.14 = (f32[256,32]{0,1:T(8,128)}, f32[256,32]{0,1:T(8,128)S(1)}, u32[]{:S(2)}) copy-start(f32[256,32]{0,1:T(8,128)S(1)} %get-tuple-element.41) | copy-start | bytes 98308
  55.4 74.8 %copy-start.16 = (f32[256,32]{0,1:T(8,128)}, f32[256,32]{0,1:T(8,128)S(1)}, u32[]{:S(2)}) copy-start(f32[256,32]{0,1:T(8,128)S(1)} %get-tuple-element.42) | copy-start | bytes 98308
  99.3 135.3 %all-gather.9.cloned.1.call-start = ((), (), s32[]{:S(2)}) async-start(), calls=%async_computation.6 | async-start | bytes 4718592 | tf_op jit(solution)/shard_map/all_gather | solution.py:117
  101.5 193.1 %all-gather.13.cloned.1.call-start = ((), (), s32[]{:S(2)}) async-start(), calls=%async_computation.8 | async-start | bytes 4325376 | tf_op jit(solution)/shard_map/all_gather | solution.py:66
  102.0 233.3 %all-gather.15.cloned.1.call-start = ((), (), s32[]{:S(2)}) async-start(), calls=%async_computation.9 | async-start | bytes 8650752 | tf_op jit(solution)/shard_map/all_gather | solution.py:67
  102.6 296.3 %all-gather.17.cloned.1.call-start = ((), (), s32[]{:S(2)}) async-start(), calls=%async_computation.10 | async-start | bytes 4325376 | tf_op jit(solution)/shard_map/all_gather | solution.py:68
  103.2 612.9 %reduce-scatter.6.cloned.1.call-start = ((), (), s32[]{:S(2)}) async-start(), calls=%async_computation.11 | async-start | bytes 9437184 | tf_op jit(solution)/shard_map/reduce_scatter | solution.py:206
  104.3 24.7 %copy-start.39 = (f32[64]{0:T(128)}, f32[64]{0:T(128)S(1)}, u32[]{:S(2)}) copy-start(f32[64]{0:T(128)S(1)} %convert_element_type.119) | copy-start | bytes 772
  131.5 61.7 %copy-start.6 = (bf16[4,256,16,32]{1,3,2,0:T(8,128)(2,1)}, bf16[4,256,16,32]{1,3,2,0:T(8,128)(2,1)S(1)}, u32[]{:S(2)}) copy-start(bf16[4,256,16,32]{1,3,2,0:T(8,128)(2,1)S(1)} %copy.61) | copy-start | bytes 3145732
  294.6 40.8 %copy-start.34 = (f32[2048]{0:T(1024)S(1)}, f32[2048]{0:T(1024)}, u32[]{:S(2)}) copy-start(f32[2048]{0:T(1024)} %convert_element_type.123) | copy-start | bytes 24580
  307.4 123.5 %copy-start.36 = (f32[1024]{0:T(1024)}, f32[1024]{0:T(1024)S(1)}, u32[]{:S(2)}) copy-start(f32[1024]{0:T(1024)S(1)} %fusion.49) | copy-start | bytes 12292
  413.4 17.5 %copy-start.29 = (f32[1,2,4,128]{3,1,2,0:T(2,128)S(1)}, f32[1,2,4,128]{3,1,2,0:T(2,128)}, u32[]{:S(2)}) copy-start(f32[1,2,4,128]{3,1,2,0:T(2,128)} %copy-done.28) | copy-start | bytes 12292
  513.8 74.3 %copy-start.7 = (bf16[4,256,16,32]{1,3,2,0:T(8,128)(2,1)S(1)}, bf16[4,256,16,32]{1,3,2,0:T(8,128)(2,1)}, u32[]{:S(2)}) copy-start(bf16[4,256,16,32]{1,3,2,0:T(8,128)(2,1)} %copy-done.6) | copy-start | bytes 3145732
  627.8 241.5 %reduce-scatter.14.cloned.1.call-start = ((), (), s32[]{:S(2)}) async-start(), calls=%async_computation.15 | async-start | bytes 8650752 | tf_op jit(solution)/shard_map/reduce_scatter | solution.py:239
  638.5 382.9 %reduce-scatter.10.cloned.1.call-start = ((), (), s32[]{:S(2)}) async-start(), calls=%async_computation.13 | async-start | bytes 8650752 | tf_op jit(solution)/shard_map/reduce_scatter | solution.py:237
  650.4 558.2 %reduce-scatter.12.cloned.1.call-start = ((), (), s32[]{:S(2)}) async-start(), calls=%async_computation.14 | async-start | bytes 17301504 | tf_op jit(solution)/shard_map/reduce_scatter | solution.py:238
  668.7 699.6 %reduce-scatter.8.cloned.1.call-start = ((), (), s32[]{:S(2)}) async-start(), calls=%async_computation.12 | async-start | bytes 12976128 | tf_op jit(solution)/shard_map/reduce_scatter | solution.py:236
  706.1 13.4 copy-start.23
  706.1 13.5 copy-start.42
  745.0 53.5 %copy-start.31 = (f32[1,2,4,128]{3,1,2,0:T(2,128)S(1)}, f32[1,2,4,128]{3,1,2,0:T(2,128)}, u32[]{:S(2)}) copy-start(f32[1,2,4,128]{3,1,2,0:T(2,128)} %copy-done.30) | copy-start | bytes 12292
  (39 other events, 198.5 us)
Sparse Core Ops, SparseCore 0:
  11.0 72.4 all-gather.6
  99.4 46.2 all-gather.10
  147.4 45.3 all-gather.8
  195.6 60.8 all-gather.12
  259.3 75.9 all-gather.14
  338.2 60.6 all-gather.16
  627.9 88.1 reduce-scatter.5
  719.0 150.2 reduce-scatter.13
  872.1 149.2 reduce-scatter.9
  1024.1 184.4 reduce-scatter.11
  1215.2 153.0 reduce-scatter.7
where the time goes:
time: 1380 us
  waiting for transfers between devices  683 us (49%)
  matrix products  421 us (31%)
  other arithmetic  108 us (8%)
  blocking collectives  81.4 us (6%)
  local copies, waits for them, and re-layouts  65.5 us (5%)
  between operations  14.8 us (1%)
    reduce_scatter x1, waiting for transfers between devices, shards(): lax.psum_scatter(grad_gateup_w, ('row', 'seq'), scatter_dimension=0, tile...  187 us
    reduce_scatter x1, waiting for transfers between devices, shards(): lax.psum_scatter(grad_qkv_w, ('row', 'seq'), scatter_dimension=0, tiled=T...  160 us
    reduce_scatter x1, waiting for transfers between devices, shards(): lax.psum_scatter(grad_out_w, ('row', 'seq'), scatter_dimension=0, tiled=T...  152 us
    unnamed x2, blocking collectives  81.4 us
    dot_general x1, matrix products, shards(): jnp.einsum('sqkgd,snkd->sqkgn', grad_heads, value_split, preferred_elemen...  74.3 us
    reduce_scatter x1, waiting for transfers between devices, shards(): lax.psum_scatter(grad_down, ('row', 'seq'), scatter_dimension=0, tiled=True)  60.4 us
    dot_general x4, matrix products, times_transposed(): lax.dot_general(left, right, (((1,), (1,)), ((), ())), preferred_element_...  55.6 us
    dot_general x1, matrix products, shards(): jnp.einsum('sqkgn,snkd->sqkgd', weights_now.astype(jnp.bfloat16), value_s...  48.3 us
  transfers between devices with their start and end apart: 11, of which 9 were waited for; matrix products, arithmetic and copies ran while one was open for 25% of the time, Pallas kernels for 0%

commit v1 on v0

v1 whole, which is shorter than its diff:
```python
import functools
import math

import jax
import jax.numpy as jnp
from jax import lax
from jax.experimental import pallas as pl
from jax.experimental.pallas import tpu as pltpu
from jax.sharding import PartitionSpec as P

norm_eps = 1e-06
theta_base = 10000.0
both = ("row", "seq")
f32 = jnp.float32
bf16 = jnp.bfloat16
vmem_cap = 56 * 1024 * 1024
NN = (((1,), (0,)), ((), ()))
NT = (((1,), (1,)), ((), ()))
TN = (((0,), (0,)), ((), ()))


def mm(left, right, dims=NN):
    return lax.dot_general(left, right, dims, preferred_element_type=f32)


def params(n_grid):
    return pltpu.CompilerParams(
        dimension_semantics=("arbitrary",) * n_grid, vmem_limit_bytes=vmem_cap
    )


def lane_iota(shape):
    return lax.broadcasted_iota(jnp.int32, shape, len(shape) - 1)


def group_matrix(head_dim, value):
    i = lax.broadcasted_iota(jnp.int32, (128, 128), 0) // head_dim
    j = lax.broadcasted_iota(jnp.int32, (128, 128), 1) // head_dim
    return jnp.where(i == j, value, 0.0).astype(bf16)


def group_sum(values, matrix):
    high = values.astype(bf16)
    low = (values - high.astype(f32)).astype(bf16)
    return mm(high, matrix) + mm(low, matrix)


def turn(values, cos_ref, sa_ref, sb_ref):
    return (
        values * cos_ref[...]
        + pltpu.roll(values, 96, 1) * sa_ref[...]
        + pltpu.roll(values, 32, 1) * sb_ref[...]
    )


def turn_back(values, cos_ref, sa_ref, sb_ref):
    return (
        values * cos_ref[...]
        - pltpu.roll(values, 96, 1) * sa_ref[...]
        - pltpu.roll(values, 32, 1) * sb_ref[...]
    )


def project_kernel(
    normed_slabs,
    head_dim,
    with_scale,
    tok_ref,
    w_ref,
    gain_ref,
    cos_ref,
    sa_ref,
    sb_ref,
    *rest,
):
    if with_scale:
        heads_ref, raw_ref, scale_ref = rest
        x = tok_ref[...].astype(f32)
        scale = lax.rsqrt(jnp.mean(x * x, axis=-1, keepdims=True) + norm_eps)
        scale_ref[...] = jnp.broadcast_to(scale, scale_ref.shape)
    else:
        scale_in_ref, heads_ref, raw_ref = rest
        scale = scale_in_ref[:, :1]
    projected = mm(tok_ref[...], w_ref[...]) * scale
    mean_matrix = group_matrix(head_dim, 1.0 / head_dim)
    raw_ref[...] = projected[:, : raw_ref.shape[1]].astype(bf16)
    for slab in range(heads_ref.shape[1] // 128):
        lanes = slice(128 * slab, 128 * slab + 128)
        part = projected[:, lanes]
        if slab < normed_slabs:
            inverse = lax.rsqrt(group_sum(part * part, mean_matrix) + norm_eps)
            part = turn(part * inverse * gain_ref[...], cos_ref, sa_ref, sb_ref)
        heads_ref[:, lanes] = part.astype(bf16)


def project(tokens, weight, gain, tables, normed, head_dim, scale=None):
    rows, width = tokens.shape
    out_width = weight.shape[1]
    span = tables[0].shape[0]
    row_block = lambda n: pl.BlockSpec((span, n), lambda i: (i, 0))
    fixed = lambda a: pl.BlockSpec(a.shape, lambda i: (0,) * a.ndim)
    args = [tokens, weight, gain, *tables]
    in_specs = [row_block(width), fixed(weight), fixed(gain)] + [fixed(t) for t in tables]
    out_shape = [
        jax.ShapeDtypeStruct((rows, out_width), bf16),
        jax.ShapeDtypeStruct((rows, normed), bf16),
    ]
    out_specs = [row_block(out_width), row_block(normed)]
    if scale is None:
        out_shape.append(jax.ShapeDtypeStruct((rows, 128), f32))
        out_specs.append(row_block(128))
    else:
        args.append(scale)
        in_specs.append(row_block(128))
    return pl.pallas_call(
        functools.partial(project_kernel, normed // 128, head_dim, scale is None),
        grid=(rows // span,),
        in_specs=in_specs,
        out_specs=out_specs,
        out_shape=out_shape,
        compiler_params=params(1),
        cost_estimate=pl.CostEstimate(
            flops=2 * rows * width * out_width,
            bytes_accessed=2 * (rows * (width + 2 * out_width) + width * out_width),
            transcendentals=rows * normed,
        ),
    )(*args)


def placed_pair(slab, parity, low):
    values = slab.astype(f32)
    rolled = pltpu.roll(values, 64, 1)
    first = jnp.where(low, jnp.where(parity == 0, values, rolled), 0.0)
    second = jnp.where(low, 0.0, jnp.where(parity == 0, rolled, values))
    return first, second


def stacked(ref):
    return jnp.concatenate([ref[0, :, :128], ref[0, :, 128:]], axis=0)


def key_blocks(info_ref, seq, base, chunk_len, span, block, backward):
    offset = info_ref[0]
    length = info_ref[1 + seq]
    whole = jnp.clip(jnp.minimum(offset + 1, length) - base, 0, chunk_len) // block
    reach = jnp.clip(jnp.minimum(offset + span, length) - base, 0, chunk_len)
    count = (reach + block - 1) // block
    alive = base >= 0
    if backward:
        alive = alive & (offset < length)
    return jnp.where(alive, whole, 0), jnp.where(alive, count, 0)


def attend_kernel(block, n_chunks, with_acc, finish, info_ref, q_ref, *refs):
    keys, refs = refs[:n_chunks], refs[n_chunks:]
    values, refs = refs[:n_chunks], refs[n_chunks:]
    if with_acc:
        acc_in, refs = refs[0], refs[1:]
    if finish:
        out_ref, log_ref, acc = refs
    else:
        (acc,) = refs
        acc = acc.at[0, 0]
    seq = pl.program_id(0)
    parity = lax.rem(pl.program_id(1), 2)
    span = q_ref.shape[1]
    low = lane_iota((block, 128)) < 64
    ones_low = jnp.where(low, 1.0, 0.0).astype(bf16)
    ones_high = jnp.where(low, 0.0, 1.0).astype(bf16)
    queries = stacked(q_ref)
    acc[...] = acc_in[0, 0] if with_acc else jnp.zeros(acc.shape, f32)

    for chunk in range(n_chunks):
        base = info_ref[1 + pl.num_programs(0) + chunk]
        chunk_len = keys[chunk].shape[1]
        whole, count = key_blocks(info_ref, seq, base, chunk_len, span, block, False)

        def step(index, masked, chunk=chunk, base=base):
            rows = pl.ds(pl.multiple_of(index * block, block), block)
            k0, k1 = placed_pair(keys[chunk][0, rows, :], parity, low)
            v0, v1 = placed_pair(values[chunk][0, rows, :], parity, low)
            k_pair = jnp.concatenate([k0, k1], axis=0).astype(bf16)
            v_pair = jnp.concatenate(
                [
                    jnp.concatenate([v0.astype(bf16), ones_low], axis=1),
                    jnp.concatenate([v1.astype(bf16), ones_high], axis=1),
                ],
                axis=0,
            )
            weights = jnp.exp2(mm(queries, k_pair, NT))
            if masked:
                shape = (2 * span, 2 * block)
                q_pos = info_ref[0] + lax.rem(lax.broadcasted_iota(jnp.int32, shape, 0), span)
                k_pos = base + index * block + lax.rem(lane_iota(shape), block)
                ok = (k_pos <= q_pos) & (k_pos < info_ref[1 + seq])
                weights = jnp.where(ok, weights, 0.0)
            acc[...] += mm(weights.astype(bf16), v_pair)

        @pl.loop(0, whole)
        def _(index):
            step(index, False)

        @pl.loop(whole, count)
        def _(index):
            step(index, True)

    if finish:
        totals = acc[:, 128:]
        heads = (acc[:, :128] / totals).astype(bf16)
        logs = jnp.log2(totals)
        out_ref[0, :, :128] = heads[:span]
        out_ref[0, :, 128:] = heads[span:]
        log_ref[0, :, :128] = logs[:span]
        log_ref[0, :, 128:] = logs[span:]


def attend(info, queries, chunks, acc=None, finish=True):
    seqs, span, width = queries.shape
    kv_heads = width // 256
    q_spec = pl.BlockSpec((1, span, 256), lambda b, h, *_: (b, 0, h))
    acc_spec = pl.BlockSpec((1, 1, 2 * span, 256), lambda b, h, *_: (b, h, 0, 0))
    acc_shape = jax.ShapeDtypeStruct((seqs, kv_heads, 2 * span, 256), f32)
    block = min(256, chunks[0].shape[1])
    key_specs = [
        pl.BlockSpec((1, c.shape[1], 128), lambda b, h, *_: (b, 0, h // 2)) for c in chunks
    ]
    value_specs = [
        pl.BlockSpec((1, c.shape[1], 128), lambda b, h, *_: (b, 0, kv_heads // 2 + h // 2))
        for c in chunks
    ]
    args = [queries, *chunks, *chunks]
    in_specs = [q_spec, *key_specs, *value_specs]
    if acc is not None:
        args.append(acc)
        in_specs.append(acc_spec)
    if finish:
        out_shape = [
            jax.ShapeDtypeStruct(queries.shape, bf16),
            jax.ShapeDtypeStruct(queries.shape, f32),
        ]
        out_specs = [q_spec, q_spec]
        scratch = [pltpu.VMEM((2 * span, 256), f32)]
    else:
        out_shape, out_specs, scratch = acc_shape, acc_spec, []
    keys = sum(c.shape[1] for c in chunks)
    return pl.pallas_call(
        functools.partial(attend_kernel, block, len(chunks), acc is not None, finish),
        grid_spec=pltpu.PrefetchScalarGridSpec(
            num_scalar_prefetch=1,
            grid=(seqs, kv_heads),
            in_specs=in_specs,
            out_specs=out_specs,
            scratch_shapes=scratch,
        ),
        out_shape=out_shape,
        compiler_params=params(2),
        cost_estimate=pl.CostEstimate(
            flops=4 * 4 * seqs * span * width * keys,
            bytes_accessed=4 * seqs * (span * width * 3 + keys * width // 2),
            transcendentals=seqs * span * width // 64 * keys,
        ),
    )(info, *args)


def attend_back_kernel(block, with_acc, finish, info_ref, q_ref, do_ref, o_ref, log_ref, k_ref, v_ref, *refs):
    if with_acc:
        acc_in, refs = refs[0], refs[1:]
    dk_ref, dv_ref, dq_ref, *refs = refs
    acc, q_wide, do_wide = refs
    seq = pl.program_id(0)
    parity = lax.rem(pl.program_id(1), 2)
    span = q_ref.shape[1]
    chunk_len = k_ref.shape[1]
    base = info_ref[1 + pl.num_programs(0)]
    whole, count = key_blocks(info_ref, seq, base, chunk_len, span, block, True)
    low = lane_iota((block, 128)) < 64
    half_lane = lax.rem(lane_iota((block, 128)), 64)
    pick_low = jnp.where(low & (half_lane < 2), 1.0, 0.0)
    pick_high = jnp.where(low | (half_lane >= 2), 0.0, 1.0)

    @pl.when(parity == 0)
    def _():
        dk_ref[...] = jnp.zeros(dk_ref.shape, dk_ref.dtype)
        dv_ref[...] = jnp.zeros(dv_ref.shape, dv_ref.dtype)

    acc[...] = acc_in[0, 0] if with_acc else jnp.zeros(acc.shape, f32)

    @pl.when(count > 0)
    def _():
        lane = lax.rem(lane_iota((2 * span, 128)), 64)

        def split(values):
            high = values.astype(bf16).astype(f32)
            rest = values - high
            return jnp.where(lane == 0, high, jnp.where(lane == 1, rest, 0.0)).astype(bf16)

        heads = stacked(do_ref)
        dots = group_sum(
            heads.astype(f32) * stacked(o_ref).astype(f32), group_matrix(64, 1.0)
        )
        do_wide[:, :128] = heads
        do_wide[:, 128:] = split(-dots)
        q_wide[:, :128] = stacked(q_ref)
        q_wide[:, 128:] = split(-stacked(log_ref))

        def step(index, masked):
            rows = pl.ds(pl.multiple_of(index * block, block), block)
            k0, k1 = placed_pair(k_ref[0, rows, :], parity, low)
            v0, v1 = placed_pair(v_ref[0, rows, :], parity, low)
            k_pair = jnp.concatenate([k0, k1], axis=0)
            k_turned = jnp.transpose(k_pair).astype(bf16)
            picks = jnp.concatenate([pick_low, pick_high], axis=0).astype(bf16)
            k_wide = jnp.concatenate([k_pair.astype(bf16), picks], axis=1)
            v_wide = jnp.concatenate(
                [jnp.concatenate([v0, v1], axis=0).astype(bf16), picks], axis=1
            )
            weights = jnp.exp2(mm(k_wide, q_wide[...], NT))
            if masked:
                shape = (2 * block, 2 * span)
                q_pos = info_ref[0] + lax.rem(lane_iota(shape), span)
                k_pos = base + index * block + lax.rem(
                    lax.broadcasted_iota(jnp.int32, shape, 0), block
                )
                ok = (k_pos <= q_pos) & (k_pos < info_ref[1 + seq])
                weights = jnp.where(ok, weights, 0.0)
            grads = (weights * mm(v_wide, do_wide[...], NT)).astype(bf16)
            both_v = mm(weights.astype(bf16), do_wide[:, :128])
            both_k = mm(grads, q_wide[:, :128]) * math.log(2.0)
            acc[...] += mm(k_turned, grads)

            def joined(pair):
                total = jnp.where(low, pair[:block] + pltpu.roll(pair[block:], 64, 1), 0.0)
                return jnp.where(parity == 0, total, pltpu.roll(total, 64, 1))

            dk_ref[0, rows, :] += joined(both_k).astype(dk_ref.dtype)
            dv_ref[0, rows, :] += joined(both_v).astype(dv_ref.dtype)

        @pl.loop(0, whole)
        def _(index):
            step(index, False)

        @pl.loop(whole, count)
        def _(index):
            step(index, True)

    if finish:
        turned = jnp.transpose(acc[...]) * 0.125
        dq_ref[0, :, :128] = turned[:span].astype(dq_ref.dtype)
        dq_ref[0, :, 128:] = turned[span:].astype(dq_ref.dtype)
    else:
        dq_ref[0, 0] = acc[...]


def attend_back(info, queries, grad_out, out, logs, chunk, acc=None, finish=True):
    seqs, span, width = queries.shape
    kv_heads = width // 256
    chunk_len = chunk.shape[1]
    q_spec = pl.BlockSpec((1, span, 256), lambda b, h, *_: (b, 0, h))
    acc_spec = pl.BlockSpec((1, 1, 128, 2 * span), lambda b, h, *_: (b, h, 0, 0))
    acc_shape = jax.ShapeDtypeStruct((seqs, kv_heads, 128, 2 * span), f32)
    block = min(256, chunk_len)
    key_spec = pl.BlockSpec((1, chunk_len, 128), lambda b, h, *_: (b, 0, h // 2))
    value_spec = pl.BlockSpec(
        (1, chunk_len, 128), lambda b, h, *_: (b, 0, kv_heads // 2 + h // 2)
    )
    args = [queries, grad_out, out, logs, chunk, chunk]
    in_specs = [q_spec] * 4 + [key_spec, value_spec]
    if acc is not None:
        args.append(acc)
        in_specs.append(acc_spec)
    grad_shape = jax.ShapeDtypeStruct((seqs, chunk_len, width // 4), bf16)
    if finish:
        dq_shape, dq_spec = jax.ShapeDtypeStruct(queries.shape, bf16), q_spec
    else:
        dq_shape, dq_spec = acc_shape, acc_spec
    return pl.pallas_call(
        functools.partial(attend_back_kernel, block, acc is not None, finish),
        grid_spec=pltpu.PrefetchScalarGridSpec(
            num_scalar_prefetch=1,
            grid=(seqs, kv_heads),
            in_specs=in_specs,
            out_specs=[key_spec, key_spec, dq_spec],
            scratch_shapes=[
                pltpu.VMEM((128, 2 * span), f32),
                pltpu.VMEM((2 * span, 256), bf16),
                pltpu.VMEM((2 * span, 256), bf16),
            ],
        ),
        out_shape=[grad_shape, grad_shape, dq_shape],
        compiler_params=params(2),
        cost_estimate=pl.CostEstimate(
            flops=10 * 4 * seqs * span * width * chunk_len,
            bytes_accessed=4 * seqs * (span * width * 4 + chunk_len * width),
            transcendentals=seqs * span * width // 64 * chunk_len,
        ),
    )(info, *args)


def unproject_kernel(
    head_dim,
    n_q,
    n_k,
    dq_ref,
    dk_ref,
    dv_ref,
    qraw_ref,
    kraw_ref,
    scale_ref,
    qg_ref,
    kg_ref,
    cos_ref,
    sa_ref,
    sb_ref,
    out_ref,
    gq_ref,
    gk_ref,
):
    @pl.when(pl.program_id(0) == 0)
    def _():
        gq_ref[...] = jnp.zeros(gq_ref.shape, f32)
        gk_ref[...] = jnp.zeros(gk_ref.shape, f32)

    scale = scale_ref[:, :1]
    mean_matrix = group_matrix(head_dim, 1.0 / head_dim)
    for slab in range(n_q + n_k):
        is_q = slab < n_q
        index = slab if is_q else slab - n_q
        lanes = slice(128 * index, 128 * index + 128)
        raw = (qraw_ref if is_q else kraw_ref)[:, lanes].astype(f32)
        grad = (dq_ref if is_q else dk_ref)[:, lanes].astype(f32)
        gain = (qg_ref if is_q else kg_ref)[...]
        inverse = lax.rsqrt(group_sum(raw * raw, mean_matrix) + norm_eps)
        unit = raw * inverse
        turned = turn_back(grad, cos_ref, sa_ref, sb_ref)
        gain_part = jnp.sum(turned * unit, axis=0, keepdims=True)
        if is_q:
            gq_ref[...] += jnp.broadcast_to(gain_part, gq_ref.shape)
        else:
            gk_ref[...] += jnp.broadcast_to(gain_part, gk_ref.shape)
        inner = turned * gain
        mean = group_sum(inner * unit, mean_matrix)
        out = inverse * (inner - unit * mean) * scale
        out_ref[:, 128 * slab : 128 * slab + 128] = out.astype(bf16)
    v_start = 128 * (n_q + n_k)
    out_ref[:, v_start:] = (dv_ref[...].astype(f32) * scale).astype(bf16)


def unproject(dq, dk, dv, qraw, kraw, scale, q_gain, k_gain, tables, head_dim):
    rows, q_width = dq.shape
    kv_width = dk.shape[1]
    span = tables[0].shape[0]
    row_block = lambda a: pl.BlockSpec((span, a.shape[1]), lambda i: (i, 0))
    fixed = lambda a: pl.BlockSpec(a.shape, lambda i: (0,) * a.ndim)
    total = q_width + 2 * kv_width
    gain_shape = jax.ShapeDtypeStruct((8, 128), f32)
    return pl.pallas_call(
        functools.partial(unproject_kernel, head_dim, q_width // 128, kv_width // 128),
        grid=(rows // span,),
        in_specs=[row_block(a) for a in (dq, dk, dv, qraw, kraw, scale)]
        + [fixed(a) for a in (q_gain, k_gain, *tables)],
        out_specs=[
            pl.BlockSpec((span, total), lambda i: (i, 0)),
            pl.BlockSpec((8, 128), lambda i: (0, 0)),
            pl.BlockSpec((8, 128), lambda i: (0, 0)),
        ],
        out_shape=[jax.ShapeDtypeStruct((rows, total), bf16), gain_shape, gain_shape],
        compiler_params=params(1),
        cost_estimate=pl.CostEstimate(
            flops=8 * 128 * rows * total,
            bytes_accessed=6 * rows * total,
            transcendentals=rows * total,
        ),
    )(dq, dk, dv, qraw, kraw, scale, q_gain, k_gain, *tables)


def shards(
    tokens, lengths, cotangent, w_qkv, w_out, w_gateup, w_down, norm_attn, norm_ffn, q_gain, k_gain
):
    seq_count, span_len, model_width = tokens.shape
    row_count = seq_count * span_len
    head_dim = q_gain.shape[0]
    half_dim = head_dim // 2
    query_width = w_out.shape[1]
    kv_width = (w_qkv.shape[1] - query_width) // 2
    hidden_width = w_down.shape[1]
    log2_scale = math.log2(math.e) * head_dim ** (-0.5)

    offset = lax.axis_index("seq") * span_len
    positions = offset + jnp.arange(span_len, dtype=jnp.int32)
    inverse = theta_base ** (-jnp.arange(half_dim, dtype=f32) * 2.0 / head_dim)
    angles = positions.astype(f32)[:, None] * inverse[None, :]
    cosine, sine = jnp.cos(angles), jnp.sin(angles)
    nothing = jnp.zeros_like(sine)
    tables = (
        jnp.concatenate([cosine] * 4, axis=1),
        jnp.concatenate([-sine, nothing] * 2, axis=1),
        jnp.concatenate([nothing, sine] * 2, axis=1),
    )
    q_gain_f = jnp.concatenate([q_gain.astype(f32)] * 2)[None, :]
    k_gain_f = jnp.concatenate([k_gain.astype(f32)] * 2)[None, :]

    attn_gain = norm_attn.astype(f32)[:, None]
    ffn_gain = norm_ffn.astype(f32)[:, None]
    qkv_shard = (w_qkv.astype(f32) * attn_gain).astype(bf16)
    gateup_shard = (w_gateup.astype(f32) * ffn_gain).astype(bf16)

    gather = lambda w: lax.all_gather(w, both, axis=0, tiled=True)
    qkv_full = gather(qkv_shard)
    q_full, kv_full = qkv_full[:, :query_width], qkv_full[:, query_width:]
    out_full = gather(w_out)
    gateup_full = gather(gateup_shard)
    down_full = gather(w_down)

    rows_in = tokens.reshape(row_count, model_width)
    kv, k_raw, scale1 = project(rows_in, kv_full, k_gain_f, tables, kv_width, head_dim)
    q, q_raw = project(
        rows_in, q_full, q_gain_f * log2_scale, tables, query_width, head_dim, scale1
    )
    q = q.reshape(seq_count, span_len, query_width)
    kv = kv.reshape(seq_count, span_len, 2 * kv_width)
    kv_all = lax.all_gather(kv, "seq", axis=1, tiled=True)
    info = jnp.concatenate(
        [offset[None].astype(jnp.int32), lengths, jnp.zeros((1,), jnp.int32)]
    )
    heads, logs = attend(info, q, [kv_all])
    attended = heads.reshape(row_count, query_width)

    inputs = rows_in.astype(f32)
    middle = inputs + mm(attended, out_full, NT)
    middle_low = middle.astype(bf16)
    scale2 = lax.rsqrt(jnp.mean(middle * middle, axis=-1, keepdims=True) + norm_eps)
    gate_up = mm(middle_low, gateup_full) * scale2
    gate, up = gate_up[:, :hidden_width], gate_up[:, hidden_width:]
    sig = jax.nn.sigmoid(gate)
    silu = gate * sig
    hidden = (silu * up).astype(bf16)
    output = (middle + mm(hidden, down_full, NT)).astype(bf16)

    valid = (positions[None, :] < lengths[:, None]).reshape(row_count, 1)
    cot = jnp.where(valid, cotangent.reshape(row_count, model_width), 0)
    grad_down = mm(cot, hidden, TN)
    grad_hidden = mm(cot, down_full)
    grad_gate = grad_hidden * up * (sig * (1.0 + gate * (1.0 - sig)))
    grad_up = grad_hidden * silu
    grad_gu = (jnp.concatenate([grad_gate, grad_up], axis=1) * scale2).astype(bf16)
    grad_gateup = mm(middle_low, grad_gu, TN)
    back2 = mm(grad_gu, gateup_full, NT)
    unit2 = middle * scale2
    grad_middle = (
        cot.astype(f32) + back2 - unit2 * jnp.mean(back2 * unit2, axis=-1, keepdims=True)
    )
    grad_branch = grad_middle.astype(bf16)
    grad_out = mm(grad_branch, attended, TN)
    grad_heads = mm(grad_branch, out_full).astype(bf16)
    grad_heads = grad_heads.reshape(seq_count, span_len, query_width)

    dk, dv, dq = attend_back(info, q, grad_heads, heads, logs, kv_all)
    dkv = lax.psum_scatter(
        jnp.concatenate([dk, dv], axis=-1), "seq", scatter_dimension=1, tiled=True
    )
    dkv = dkv.reshape(row_count, 2 * kv_width)
    grad_proj, gq, gk = unproject(
        dq.reshape(row_count, query_width),
        dkv[:, :kv_width],
        dkv[:, kv_width:],
        q_raw,
        k_raw,
        scale1,
        q_gain_f,
        k_gain_f,
        tables,
        head_dim,
    )
    grad_qkv = mm(rows_in, grad_proj, TN)
    back1 = mm(grad_proj, qkv_full, NT)
    unit1 = inputs * scale1[:, :1]
    grad_tokens = (
        grad_middle + back1 - unit1 * jnp.mean(back1 * unit1, axis=-1, keepdims=True)
    ).astype(bf16)

    scatter = lambda g: lax.psum_scatter(
        g.astype(bf16), both, scatter_dimension=0, tiled=True
    ).astype(f32)
    sum_down = scatter(grad_down)
    sum_gateup = scatter(grad_gateup)
    sum_out = scatter(grad_out)
    sum_qkv = scatter(grad_qkv)
    gains = lax.psum(jnp.concatenate([gq[:1], gk[:1]], axis=0), both)
    gains = gains[:, :head_dim] + gains[:, head_dim:]
    return (
        output.reshape(tokens.shape),
        grad_tokens.reshape(tokens.shape),
        sum_qkv * attn_gain,
        sum_out,
        sum_gateup * ffn_gain,
        sum_down,
        jnp.sum(sum_qkv * w_qkv.astype(f32), axis=1),
        jnp.sum(sum_gateup * w_gateup.astype(f32), axis=1),
        gains[0],
        gains[1],
    )


def solution(mesh):
    rows = P("row", "seq", None)
    weight = P(both, None)
    vector = P(both)
    return jax.shard_map(
        shards,
        mesh=mesh,
        in_specs=(rows, P("row"), rows, weight, weight, weight, weight, vector, vector, P(), P()),
        out_specs=(rows, rows, weight, weight, weight, weight, vector, vector, P(), P()),
        check_vma=False,
    )
```

time: 1380 us -> 1180 us (0.86); the launches traced: 1380 us -> 1190 us
  matrix products: 421 us -> 134 us
  waiting for transfers between devices: 683 us -> 862 us
  Pallas kernels: 0 us -> 75.5 us
  other arithmetic: 108 us -> 46.8 us
  local copies, waits for them, and re-layouts: 65.5 us -> 18.4 us
  blocking collectives: 81.4 us -> 37.5 us
    dot_general x18 -> x11, matrix products: 421 us -> 134 us  [mm(): return lax.dot_general(left, right, dims, preferred_element_type=f32)]
    all_gather x6 -> x5, waiting for transfers between devices: 111 us -> 285 us  [the longest x4 230 us: shards(): gather = lambda w: lax.all_gather(w, both, axis=0, tiled=True)]
    unnamed x2 -> x0, blocking collectives: 81.4 us -> none
    pallas_call x0 -> x5, Pallas kernels: none -> 75.5 us  [the longest x1 28.5 us: attend_back(): pl.pallas_call(functools.partial(attend_back_kernel, block, acc is not No...]
    reduce_sum x7 -> x2, other arithmetic: 55.4 us -> 4.86 us  [the longest x1 2.47 us: shards(): jnp.sum(sum_gateup * w_gateup.astype(f32), axis=1)]
    psum x0 -> x1, blocking collectives: none -> 37.5 us  [shards(): gains = lax.psum(jnp.concatenate([gq[:1], gk[:1]], axis=0), both)]
    reshape x5 -> x0, local copies, waits for them, and re-layouts: 22.6 us -> none  [the longest x2 15.5 us: shards(): grad_attended.reshape(seq_count, span_len, kv_heads, group_size, head_dim)]
  transfers between devices with their start and end apart: 11 -> 10, of which waited for: 9 -> 10; matrix products, arithmetic and copies ran while one was open for 25% -> 11% of each run, Pallas kernels for 0% -> 3%
where the time goes in v1:
time: 1180 us; the launch traced here: 1190 us
  waiting for transfers between devices  862 us (73%)
  matrix products  134 us (11%)
  Pallas kernels  75.5 us (6%)
  other arithmetic  46.8 us (4%)
  blocking collectives  37.5 us (3%)
  local copies, waits for them, and re-layouts  18.4 us (2%)
  between operations  14.8 us (1%)
    reduce_scatter x4, waiting for transfers between devices, shards(): lax.psum_scatter(g.astype(bf16), both, scatter_dimension=0, tiled=True)  453 us
    all_gather x4, waiting for transfers between devices, shards(): gather = lambda w: lax.all_gather(w, both, axis=0, tiled=True)  230 us
    dot_general x11, matrix products, mm(): return lax.dot_general(left, right, dims, preferred_element_type=f32)  134 us
    reduce_scatter x1, waiting for transfers between devices, shards(): lax.psum_scatter(jnp.concatenate([dk, dv], axis=-1), 'seq', scatter_dimen...  122 us
    all_gather x1, waiting for transfers between devices, shards(): kv_all = lax.all_gather(kv, 'seq', axis=1, tiled=True)  54.9 us
    psum x1, blocking collectives, shards(): gains = lax.psum(jnp.concatenate([gq[:1], gk[:1]], axis=0), both)  37.5 us
    pallas_call x1, Pallas kernels, attend_back(): pl.pallas_call(functools.partial(attend_back_kernel, block, acc is not No...  28.5 us
  transfers between devices with their start and end apart: 10, of which 10 were waited for; matrix products, arithmetic and copies ran while one was open for 11% of the time, Pallas kernels for 3%

profile of v1, /device:TPU:0, one launch (start us, length us, event | category | flops | bytes accessed | tf_op | source)
XLA Modules:
  0.0 1189.4 jit_solution(14945772879206941284)
XLA Ops:
  13.8 69.9 %all-gather.6.cloned.1.call-done = bf16[2048,1536]{1,0:T(8,128)(2,1)} async-done(((bf16[64,1536]{1,0:T(8,128)(2,1)}), bf16[2048,1536]{1,0:T(8,128)(2,1)}) %all-gather.6.cloned.1.call-update) | async-done | bytes 6291472 | tf_op jit(solution)/shard_map/all_gather | solution.py:507
  109.1 11.2 shard_map.187
  120.3 54.9 %all-gather.8.cloned.1.call-done.refs_0_.refs_1_.k_ref.v_ref = bf16[4,2048,512]{2,1,0:T(8,128)(2,1)} async-done(((bf16[4,256,512]{2,1,0:T(8,128)(2,1)}), bf16[4,2048,512]{2,1,0:T(8,128)(2,1)}) %all-gather.8.cloned.1.call-update) | async-done | bytes 8388624 | tf_op jit(solution)/shard_map/all_gather | solution.py:521
  175.2 19.1 %shard_map.188 = (bf16[4,256,1024]{2,1,0:T(8,128)(2,1)}, f32[4,256,1024]{2,1,0:T(8,128)}) custom-call(s32[6]{0:T(128)} %pad_add_fusion.info_ref, bf16[4,256,1024]{2,1,0:T(8,128)(2,1)} %bitcast.58, bf16[4,2048,512]{2,1,0:T(8,128)(2,1)} %all-gather.8.cloned.1.call-done.refs_0_.refs_1_.k_ref.v_ref, ...), custom_call_target="tpu_custom_call" | custom-call | flops 34359738368 | bytes 29360128 | tf_op jit(solution)/shard_map/pallas_call | solution.py:246
  194.3 44.6 %all-gather.10.cloned.1.call-done = bf16[2048,1024]{1,0:T(8,128)(2,1)} async-done(((bf16[64,1024]{1,0:T(8,128)(2,1)}), bf16[2048,1024]{1,0:T(8,128)(2,1)}) %all-gather.10.cloned.1.call-update) | async-done | bytes 4194320 | tf_op jit(solution)/shard_map/all_gather | solution.py:507
  238.9 11.9 %multiply_reduce_fusion.1 = (f32[1024]{0:T(1024)S(1)}, f32[1024,2048]{1,0:T(8,128)}) fusion(bf16[1024,1024]{1,0:T(8,128)(2,1)} %bitcast.56, bf16[2048,1024]{1,0:T(8,128)(2,1)} %all-gather.10.cloned.1.call-done, bf16[1024,2048]{1,0:T(8,128)(2,1)} %bitcast.49), kind=kOutput, calls=%fused_computation.13 | convolution fusion | flops 4303354880 | bytes 18878464 | tf_op jit(solution)/shard_map/dot_general | solution.py:23
  250.9 67.3 %all-gather.12.cloned.1.call-done = bf16[2048,2048]{1,0:T(8,128)(2,1)} async-done(((bf16[64,2048]{1,0:T(8,128)(2,1)}), bf16[2048,2048]{1,0:T(8,128)(2,1)}) %all-gather.12.cloned.1.call-update) | async-done | bytes 8388624 | tf_op jit(solution)/shard_map/all_gather | solution.py:507
  318.2 15.8 %convolution_multiply_fusion = f32[1024,2048]{1,0:T(8,128)} fusion(bf16[2048,2048]{1,0:T(8,128)(2,1)} %all-gather.12.cloned.1.call-done, f32[1024]{0:T(1024)S(1)} %add_rsqrt_fusion, f32[1024,2048]{1,0:T(8,128)} %get-tuple-element.55), kind=kOutput, calls=%fused_computation.17 | convolution fusion | flops 8594128896 | bytes 25169920 | tf_op jit(solution)/shard_map/dot_general | solution.py:23
  334.0 47.8 %all-gather.14.cloned.1.call-done = bf16[2048,1024]{1,0:T(8,128)(2,1)} async-done(((bf16[64,1024]{1,0:T(8,128)(2,1)}), bf16[2048,1024]{1,0:T(8,128)(2,1)}) %all-gather.14.cloned.1.call-update) | async-done | bytes 4194320 | tf_op jit(solution)/shard_map/all_gather | solution.py:507
  381.8 15.8 %multiply_multiply_fusion = (f32[1024,1024]{1,0:T(8,128)}, f32[1024,1024]{1,0:T(8,128)}, bf16[1024,1024]{1,0:T(8,128)(2,1)}) fusion(f32[1024,2048]{1,0:T(8,128)} %convolution_multiply_fusion, bf16[1024,2048]{1,0:T(8,128)(2,1)} %bitcast_select_fusion, bf16[2048,1024]{1,0:T(8,128)(2,1)} %all-gather.14.cloned.1.call-done), kind=kOutput, calls=%fused_computation.19 | convolution fusion | flops 4308598784 | bytes 27262976 | tf_op jit(solution)/shard_map/dot_general | solution.py:23
  397.6 17.4 %multiply_reduce_fusion = (f32[1024]{0:T(1024)S(1)}, f32[1024,2048]{1,0:T(8,128)}) fusion(f32[1024,2048]{1,0:T(8,128)} %get-tuple-element.55, f32[1024]{0:T(1024)S(1)} %add_rsqrt_fusion, bf16[2048,2048]{1,0:T(8,128)(2,1)} %all-gather.12.cloned.1.call-done, f32[1024,1024]{1,0:T(8,128)} %get-tuple-element.37, f32[1024,1024]{1,0:T(8,128)} %get-tuple-element.36), kind=kOutput, calls=%fused_computation.11 | convolution fusion | flops 8602516480 | bytes 33562624 | tf_op jit(solution)/shard_map/dot_general | solution.py:23
  428.0 28.5 %shard_map.189 = (bf16[4,2048,256]{2,1,0:T(8,128)(2,1)}, bf16[4,2048,256]{2,1,0:T(8,128)(2,1)}, bf16[4,256,1024]{2,1,0:T(8,128)(2,1)}) custom-call(s32[6]{0:T(128)} %pad_add_fusion.info_ref, bf16[4,256,1024]{2,1,0:T(8,128)(2,1)} %bitcast.59, bf16[4,256,1024]{2,1,0:T(8,128)(2,1)} %bitcast.60, bf16[4,256,1024]{2,1,0:T(8,128)(2,1)} %get-tuple-element.26.o_ref, ...), custom_call_target="tpu_custom_call" | custom-call | flops 85899345920 | bytes 50331648 | tf_op jit(solution)/shard_map/pallas_call | solution.py:376
  475.3 9.5 convolution_convert_fusion.3
  484.9 16.2 %convolution_convert_fusion = bf16[2048,2048]{1,0:T(8,128)(2,1)} fusion(f32[1024,2048]{1,0:T(8,128)} %get-tuple-element.55, f32[1024,1024]{1,0:T(8,128)} %get-tuple-element.37, f32[1024,1024]{1,0:T(8,128)} %get-tuple-element.36, f32[1024]{0:T(1024)S(1)} %add_rsqrt_fusion), kind=kOutput, calls=%fused_computation.14 | convolution fusion | flops 8602517504 | bytes 25169920 | tf_op jit(solution)/shard_map/dot_general | solution.py:23
  502.3 122.4 %reduce-scatter.6.cloned.1.call-done = bf16[4,256,512]{2,1,0:T(8,128)(2,1)} async-done(((bf16[4,2048,512]{2,1,0:T(8,128)(2,1)}), bf16[4,256,512]{2,1,0:T(8,128)(2,1)}) %reduce-scatter.6.cloned.1.call-update) | async-done | bytes 1048592 | tf_op jit(solution)/shard_map/reduce_scatter | solution.py:558
  636.2 10.6 fusion.6
  648.6 9.7 add_convert_fusion
  658.3 109.9 %reduce-scatter.14.cloned.1.call-done = bf16[64,1024]{1,0:T(8,128)(2,1)} async-done(((bf16[2048,1024]{1,0:T(8,128)(2,1)}), bf16[64,1024]{1,0:T(8,128)(2,1)}) %reduce-scatter.14.cloned.1.call-update) | async-done | bytes 131088 | tf_op jit(solution)/shard_map/reduce_scatter | solution.py:581
  769.8 140.4 %reduce-scatter.10.cloned.1.call-done = bf16[64,1024]{1,0:T(8,128)(2,1)} async-done(((bf16[2048,1024]{1,0:T(8,128)(2,1)}), bf16[64,1024]{1,0:T(8,128)(2,1)}) %reduce-scatter.10.cloned.1.call-update) | async-done | bytes 131088 | tf_op jit(solution)/shard_map/reduce_scatter | solution.py:581
  913.2 37.5 %psum.7 = f32[2,128]{1,0:T(2,128)S(1)} all-reduce(f32[2,128]{1,0:T(2,128)S(1)} %pad_maximum_fusion.4), channel_id=1, replica_groups=mesh['row'=4,'seq'=8] {'row','seq'}, use_global_device_ids=true, to_apply=%region_10.11 | all-reduce | flops 256 | bytes 2048 | tf_op jit(solution)/shard_map/psum | solution.py:588
  951.4 12.6 %fusion.2 = (f32[1024]{0:T(1024)S(1)}, f32[1024,2048]{1,0:T(8,128)}) fusion(f32[1024]{0:T(1024)S(1)} %slice_reduce_fusion, bf16[4,256,2048]{2,1,0:T(8,128)(2,1)} %param.11, bf16[1024,1536]{1,0:T(8,128)(2,1)} %get-tuple-element.33, bf16[2048,1536]{1,0:T(8,128)(2,1)} %all-gather.6.cloned.1.call-done), kind=kOutput, calls=%fused_computation.4 | convolution fusion | flops 6450838528 | bytes 22028288 | tf_op jit(solution)/shard_map/dot_general | solution.py:23
  964.0 98.3 %reduce-scatter.12.cloned.1.call-done = bf16[64,2048]{1,0:T(8,128)(2,1)} async-done(((bf16[2048,2048]{1,0:T(8,128)(2,1)}), bf16[64,2048]{1,0:T(8,128)(2,1)}) %reduce-scatter.12.cloned.1.call-update) | async-done | bytes 262160 | tf_op jit(solution)/shard_map/reduce_scatter | solution.py:581
  1064.8 10.2 fusion.4
  1075.0 104.8 %reduce-scatter.8.cloned.1.call-done = bf16[64,1536]{1,0:T(8,128)(2,1)} async-done(((bf16[2048,1536]{1,0:T(8,128)(2,1)}), bf16[64,1536]{1,0:T(8,128)(2,1)}) %reduce-scatter.8.cloned.1.call-update) | async-done | bytes 196624 | tf_op jit(solution)/shard_map/reduce_scatter | solution.py:581
  (98 shorter events, 88.2 us)
Async XLA Ops:
  7.2 76.6 %all-gather.6.cloned.1.call-start = ((), (), s32[]{:S(2)}) async-start(), calls=%async_computation.5 | async-start | bytes 6488064 | tf_op jit(solution)/shard_map/all_gather | solution.py:507
  10.1 165.1 %all-gather.8.cloned.1.call-start = ((), (), s32[]{:S(2)}) async-start(), calls=%async_computation.6 | async-start | bytes 9437184 | tf_op jit(solution)/shard_map/all_gather | solution.py:521
  86.8 8.4 copy-start.13
  86.8 9.0 copy-start.4
  86.8 10.9 copy-start.11
  86.8 11.0 copy-start.14
  94.4 144.5 %all-gather.10.cloned.1.call-start = ((), (), s32[]{:S(2)}) async-start(), calls=%async_computation.7 | async-start | bytes 4325376 | tf_op jit(solution)/shard_map/all_gather | solution.py:507
  95.1 223.1 %all-gather.12.cloned.1.call-start = ((), (), s32[]{:S(2)}) async-start(), calls=%async_computation.8 | async-start | bytes 8650752 | tf_op jit(solution)/shard_map/all_gather | solution.py:507
  96.6 285.2 %all-gather.14.cloned.1.call-start = ((), (), s32[]{:S(2)}) async-start(), calls=%async_computation.9 | async-start | bytes 4325376 | tf_op jit(solution)/shard_map/all_gather | solution.py:507
  97.2 527.5 %reduce-scatter.6.cloned.1.call-start = ((), (), s32[]{:S(2)}) async-start(), calls=%async_computation.10 | async-start | bytes 9437184 | tf_op jit(solution)/shard_map/reduce_scatter | solution.py:558
  397.6 17.4 %copy-start.1 = (bf16[4,256,2048]{2,1,0:T(8,128)(2,1)S(1)}, bf16[4,256,2048]{2,1,0:T(8,128)(2,1)}, u32[]{:S(2)}) copy-start(bf16[4,256,2048]{2,1,0:T(8,128)(2,1)} %param.13) | copy-start | bytes 12582916
  415.1 7.1 copy-start.12
  422.1 5.8 copy-start
  463.8 304.4 %reduce-scatter.14.cloned.1.call-start = ((), (), s32[]{:S(2)}) async-start(), calls=%async_computation.14 | async-start | bytes 4325376 | tf_op jit(solution)/shard_map/reduce_scatter | solution.py:581
  473.7 1.6 copy-start.15
  473.8 436.5 %reduce-scatter.10.cloned.1.call-start = ((), (), s32[]{:S(2)}) async-start(), calls=%async_computation.12 | async-start | bytes 4325376 | tf_op jit(solution)/shard_map/reduce_scatter | solution.py:581
  484.9 577.5 %reduce-scatter.12.cloned.1.call-start = ((), (), s32[]{:S(2)}) async-start(), calls=%async_computation.13 | async-start | bytes 8650752 | tf_op jit(solution)/shard_map/reduce_scatter | solution.py:581
  501.1 678.6 %reduce-scatter.8.cloned.1.call-start = ((), (), s32[]{:S(2)}) async-start(), calls=%async_computation.11 | async-start | bytes 6488064 | tf_op jit(solution)/shard_map/reduce_scatter | solution.py:581
  624.7 11.5 copy-start.2
  646.8 1.8 copy-start.18
  951.4 111.0 %copy-start.5 = (bf16[64,2048]{1,0:T(8,128)(2,1)S(1)}, bf16[64,2048]{1,0:T(8,128)(2,1)}, u32[]{:S(2)}) copy-start(bf16[64,2048]{1,0:T(8,128)(2,1)} %param.16) | copy-start | bytes 786436
  951.4 111.0 %copy-start.8 = (f32[64]{0:T(128)S(1)}, f32[64]{0:T(128)}, u32[]{:S(2)}) copy-start(f32[64]{0:T(128)} %copy-done.7) | copy-start | bytes 772
  1064.8 114.9 %copy-start.6 = (bf16[64,1536]{1,0:T(8,128)(2,1)S(1)}, bf16[64,1536]{1,0:T(8,128)(2,1)}, u32[]{:S(2)}) copy-start(bf16[64,1536]{1,0:T(8,128)(2,1)} %param.14) | copy-start | bytes 589828
  1064.8 114.9 %copy-start.10 = (f32[64]{0:T(128)S(1)}, f32[64]{0:T(128)}, u32[]{:S(2)}) copy-start(f32[64]{0:T(128)} %copy-done.9) | copy-start | bytes 772
  (5 other events, 4.3 us)
Sparse Core Ops, SparseCore 0:
  11.6 72.1 all-gather.5
  94.5 80.6 all-gather.7
  178.2 60.6 all-gather.9
  242.3 75.8 all-gather.11
  321.0 60.6 all-gather.13
  463.9 160.7 reduce-scatter.5
  627.0 141.1 reduce-scatter.13
  771.1 139.1 reduce-scatter.9
  912.6 149.7 reduce-scatter.11
  1067.8 111.8 reduce-scatter.7
